TPU v7x, 256 devices: a whole 4x4x8 slice. The times are simulated.
256 devices in a mesh: gx: 16 (over x, y_hi, core), gy: 16 (over y_lo, z).
Axes of the slice: x: 4, y: 4 (y_hi: 2, y_lo: 2; y = y_hi * 2 + y_lo), z: 8, core: 2. Of those that a mesh axis runs over, the one named last changes fastest.
Arguments:
- stencil: float32 [3, 3, 3, 64, 512, 512], P(None, None, None, 'gx', 'gy'), may hold values from -1 to 30, as said below
Outputs:
- level_one: float32 [3, 3, 3, 32, 256, 512], P(None, None, None, 'gx', 'gy')
- level_two: float32 [3, 3, 3, 16, 128, 512], P(None, None, None, 'gx', 'gy')
Inputs may be any that keep to these rules, and one draw needn't show every extreme that they name: `stencil`: the centre coefficient (offset index 1, 1, 1) of every cell exceeds the sum of magnitudes of its 26 other coefficients; the others are not positive.
All inputs are finite; a program needn't handle non-finite values.
Results may differ from a plain program's by a relative error of at most 0.00002.
Values sent between devices are 32-bit elements; how exact they have to be, the bound alone decides.
A program may use at most 128 MiB of HBM per device.

v0:
```python
import jax
import jax.numpy as jnp
from jax import lax
from jax.sharding import PartitionSpec as P


def from_behind(value, axis, steps):
    count = lax.axis_size(axis)
    initial, last = (max(0, -steps), min(count, count - steps))
    return lax.ppermute(value, axis, [(source, source + steps) for source in range(initial, last)])


def boundary_mask(coeffs, x_start, y_start, x_total, y_total):
    shape = coeffs.shape
    off_x = lax.broadcasted_iota(jnp.int32, shape, 0) - 1
    off_y = lax.broadcasted_iota(jnp.int32, shape, 1) - 1
    off_z = lax.broadcasted_iota(jnp.int32, shape, 2) - 1
    cell_x = lax.broadcasted_iota(jnp.int32, shape, 3) + x_start
    cell_y = lax.broadcasted_iota(jnp.int32, shape, 4) + y_start
    cell_z = lax.broadcasted_iota(jnp.int32, shape, 5)
    inside = (cell_x >= 0) & (cell_x < x_total) & (cell_y >= 0) & (cell_y < y_total)
    inside = inside & (cell_x + off_x >= 0) & (cell_x + off_x < x_total)
    inside = inside & (cell_y + off_y >= 0) & (cell_y + off_y < y_total)
    inside = inside & (cell_z + off_z >= 0) & (cell_z + off_z < shape[5])
    return jnp.where(inside, coeffs, jnp.zeros_like(coeffs))


def weight_of(shift):
    return 1.0 if shift == 0 else 0.5


def coarsen_pairs(block, before_row, odim, sdim):
    shape = block.shape
    half = shape[sdim] // 2
    paired = block.reshape(shape[:sdim] + (half, 2) + shape[sdim + 1 :])
    even_rows = lax.index_in_dim(paired, 0, sdim + 1, keepdims=False)
    odd_rows = lax.index_in_dim(paired, 1, sdim + 1, keepdims=False)
    if half > 1:
        prior = jnp.concatenate(
            [before_row, lax.slice_in_dim(odd_rows, 0, half - 1, 1, sdim)], axis=sdim
        )
    else:
        prior = before_row
    fine_rows = {-1: prior, 0: even_rows, 1: odd_rows}
    results = []
    for o in (-1, 0, 1):
        total = None
        for s in (-1, 0, 1):
            for a in (-1, 0, 1):
                m = a + s - 2 * o
                if abs(m) <= 1:
                    term = (
                        weight_of(a)
                        * weight_of(m)
                        * lax.index_in_dim(fine_rows[a], s + 1, odim, keepdims=False)
                    )
                    total = term if total is None else total + term
        results.append(total)
    return jnp.stack(results, axis=odim)


def last_rows(values, dim, width):
    length = values.shape[dim]
    return lax.slice_in_dim(values, length - width, length, 1, dim)


def rows_of(values, dim, start, stop):
    return lax.slice_in_dim(values, start, stop, 1, dim)


def shards(stencil):
    cells_x = stencil.shape[3]
    cells_y = stencil.shape[4]
    x_total = cells_x * lax.axis_size("gx")
    y_total = cells_y * lax.axis_size("gy")
    x_pos = lax.axis_index("gx") * cells_x
    y_pos = lax.axis_index("gy") * cells_y
    fine = boundary_mask(stencil, x_pos, y_pos, x_total, y_total)
    arrived_x = from_behind(last_rows(fine, 3, 1), "gx", 1)
    partial_value = coarsen_pairs(fine, arrived_x, 0, 3)
    strip = jnp.concatenate([last_rows(arrived_x, 4, 1), last_rows(fine, 4, 1)], axis=3)
    arrived_y = from_behind(strip, "gy", 1)
    partial_rim = coarsen_pairs(
        rows_of(arrived_y, 3, 1, arrived_y.shape[3]), rows_of(arrived_y, 3, 0, 1), 0, 3
    )
    coarse = coarsen_pairs(partial_value, partial_rim, 1, 4)
    level_one = boundary_mask(coarse, x_pos // 2, y_pos // 2, x_total // 2, y_total // 2)
    arrived_x = from_behind(last_rows(level_one, 3, 1), "gx", 1)
    strip = jnp.concatenate([last_rows(arrived_x, 4, 1), last_rows(level_one, 4, 1)], axis=3)
    arrived_y = from_behind(strip, "gy", 1)
    upper = coarsen_pairs(level_one, arrived_x, 0, 3)
    upper_rim = coarsen_pairs(
        rows_of(arrived_y, 3, 1, arrived_y.shape[3]), rows_of(arrived_y, 3, 0, 1), 0, 3
    )
    level_two = coarsen_pairs(upper, upper_rim, 1, 4)
    level_two = boundary_mask(level_two, x_pos // 4, y_pos // 4, x_total // 4, y_total // 4)
    return (level_one, level_two)


def solution(mesh):
    in_specs = (P(None, None, None, "gx", "gy", None),)
    out_specs = (P(None, None, None, "gx", "gy", None), P(None, None, None, "gx", "gy", None))
    return jax.shard_map(shards, mesh=mesh, in_specs=in_specs, out_specs=out_specs, check_vma=False)
```

profile of v0, /device:TPU:6, one launch (start us, length us, event | category | flops | bytes accessed | tf_op | source)
XLA Modules:
  0.0 100.7 jit_solution(16829247801775563846)
XLA Ops:
  0.7 10.6 %copy_select_fusion = f32[3,3,3,4,32,512]{5,0,4,3,2,1:T(4,128)S(1)} fusion(f32[3,3,3,4,32,512]{5,4,3,2,1,0:T(8,128)} %param.1, s32[3]{0:T(128)S(1)} %iota_add_fusion.6, s32[32]{0:T(128)S(1)} %iota_add_fusion.4, s32[4]{0:T(128)S(1)} %iota_add_fusion.5, pred[32]{0:T(512)(128)(4,1)S(1)} %get-tuple-element.24, pred[32]{0:T(512)(128)(4,1)S(1)} %get-tuple-element.25, ...), kind=kLoop, calls=%fused_computation.4 | loop fusion | flops 31850496 | bytes 14156000 | tf_op jit(solution)/shard_map/jit(_where)/select_n | solution.py:25
  11.3 2.2 %slice.374 = f32[3,3,3,1,32,512]{5,0,4,3,2,1:T(4,128)} slice(f32[3,3,3,4,32,512]{5,0,4,3,2,1:T(4,128)S(1)} %copy_select_fusion), slice={[0:3], [0:3], [0:3], [3:4], [0:32], [0:512]} | slice | bytes 3538944 | tf_op jit(solution)/shard_map/slice | solution.py:64
  13.5 1.9 %collective-permute-start = (f32[3,3,3,1,32,512]{5,0,4,3,2,1:T(4,128)}, f32[3,3,3,1,32,512]{5,0,4,3,2,1:T(4,128)}, u32[]{:S(2)}, u32[]{:S(2)}) collective-permute-start(f32[3,3,3,1,32,512]{5,0,4,3,2,1:T(4,128)} %slice.374), channel_id=1, source_target_pairs={{0,16},{16,32},{32,48},{48,64},{64,80},{80,96},{96,112},{112,128},... | collective-permute-start | bytes 5308424 | tf_op jit(solution)/shard_map/ppermute | solution.py:10
  15.7 3.2 %slice_bitcast_fusion = f32[3,3,3,2,32,512]{5,0,4,3,2,1:T(4,128)S(1)} fusion(f32[3,3,3,2,2,32,512]{6,0,5,4,3,2,1:T(4,128)} %bitcast.261), kind=kLoop, calls=%fused_computation.14 | loop fusion | bytes 7077888 | tf_op jit(solution)/shard_map/squeeze | solution.py:37
  18.9 0.6 slice.388
  19.6 7.3 %fusion.24 = f32[1,3,3,2,1,32,512]{6,0,5,4,3,2,1:T(1,128)S(1)} fusion(f32[3,3,3,2,2,32,512]{6,0,5,4,3,2,1:T(4,128)} %bitcast.262), kind=kLoop, calls=%fused_computation.52 | loop fusion | flops 1474560 | bytes 4718592 | tf_op jit(solution)/shard_map/add | solution.py:57
  26.9 23.4 %collective-permute-done = f32[3,3,3,1,32,512]{5,0,4,3,2,1:T(4,128)} collective-permute-done((f32[3,3,3,1,32,512]{5,0,4,3,2,1:T(4,128)}, f32[3,3,3,1,32,512]{5,0,4,3,2,1:T(4,128)}, u32[]{:S(2)}, u32[]{:S(2)}) %collective-permute-start) | collective-permute-done | bytes 1769504 | tf_op jit(solution)/shard_map/ppermute | solution.py:10
  50.3 0.9 slice.375
  51.3 1.3 %collective-permute-start.1 = (f32[3,3,3,5,1,512]{5,0,4,3,2,1:T(4,128)S(1)}, f32[3,3,3,5,1,512]{5,0,4,3,2,1:T(4,128)S(1)}, u32[]{:S(2)}, u32[]{:S(2)}) collective-permute-start(f32[3,3,3,5,1,512]{5,0,4,3,2,1:T(4,128)S(1)} %pad_maximum_fusion.4), channel_id=1, source_target_pairs={{0,1},{1,2},{2,3},{3,4},{4,5},{5,6},{6,7},{7,8},{8,9},{9,10},{10,1... | collective-permute-start | bytes 829448 | tf_op jit(solution)/shard_map/ppermute | solution.py:10
  52.6 13.5 %bitcast_add_fusion = (f32[1,3,3,2,32,512]{5,0,4,3,2,1:T(1,128)S(1)}, f32[1,3,3,2,32,512]{5,0,4,3,2,1:T(1,128)S(1)}) fusion(f32[3,3,3,1,32,512]{5,0,4,3,2,1:T(4,128)S(1)} %slice.388, f32[3,3,3,1,32,512]{5,0,4,3,2,1:T(4,128)} %collective-permute-done, f32[3,3,3,2,2,32,512]{6,0,5,4,3,2,1:T(4,128)} %bitcast.263), kind=kLoop, calls=%fused_computation.71 | loop fusion | flops 5308416 | bytes 11796480 | tf_op jit(solution)/shard_map/add | solution.py:57
  66.8 0.4 slice_bitcast_fusion.1
  68.2 0.8 fusion.40
  69.0 0.5 copy_select_fusion.1
  69.5 1.1 %slice.408 = f32[3,3,3,1,16,512]{5,4,3,2,1,0:T(8,128)} slice(f32[3,3,3,2,16,512]{5,4,3,2,1,0:T(8,128)S(1)} %copy_select_fusion.1), slice={[0:3], [0:3], [0:3], [1:2], [0:16], [0:512]} | slice | bytes 1769472 | tf_op jit(solution)/shard_map/slice | solution.py:64
  70.6 1.9 %collective-permute-start.2 = (f32[3,3,3,1,16,512]{5,4,3,2,1,0:T(8,128)}, f32[3,3,3,1,16,512]{5,4,3,2,1,0:T(8,128)}, u32[]{:S(2)}, u32[]{:S(2)}) collective-permute-start(f32[3,3,3,1,16,512]{5,4,3,2,1,0:T(8,128)} %slice.408), channel_id=1, source_target_pairs={{0,16},{16,32},{32,48},{48,64},{64,80},{80,96},{96,112},{112,128},... | collective-permute-start | bytes 2654216 | tf_op jit(solution)/shard_map/ppermute | solution.py:10
  72.6 0.5 iota_add_fusion.3
  73.1 0.5 compare_and_fusion
  73.6 0.6 add_compare_fusion.12
  74.2 0.8 slice.410
  74.9 1.2 %maximum_select_fusion = f32[3,3,3,1,2,16,512]{6,5,2,1,4,3,0:T(8,128)S(1)} fusion(f32[3,1,3,1,2,16,512]{6,5,2,1,4,3,0:T(8,128)S(1)} %bitcast.267, f32[3,1,3,1,2,16,512]{6,5,2,1,4,3,0:T(8,128)S(1)} %bitcast.266, f32[3,1,3,1,2,16,512]{6,5,2,1,4,3,0:T(8,128)S(1)} %bitcast.265, s32[3]{0:T(128)S(1)} %iota_add_fusion.6, s32[16]{0:T(128)S(1)} %iota_add_fusion.7, ...), kind=kLoop, calls=%fused_computation.28 | loop fusion | flops 8847360 | bytes 3539062 | tf_op jit(solution)/shard_map/jit(_where)/select_n | solution.py:25
  76.2 0.3 add.631
  76.5 12.9 %collective-permute-done.2 = f32[3,3,3,1,16,512]{5,4,3,2,1,0:T(8,128)} collective-permute-done((f32[3,3,3,1,16,512]{5,4,3,2,1,0:T(8,128)}, f32[3,3,3,1,16,512]{5,4,3,2,1,0:T(8,128)}, u32[]{:S(2)}, u32[]{:S(2)}) %collective-permute-start.2) | collective-permute-done | bytes 884768 | tf_op jit(solution)/shard_map/ppermute | solution.py:10
  89.5 1.1 %slice.409 = f32[3,3,3,1,1,512]{5,4,3,2,1,0:T(1,128)S(1)} slice(f32[3,3,3,1,16,512]{5,4,3,2,1,0:T(8,128)} %collective-permute-done.2), slice={[0:3], [0:3], [0:3], [0:1], [15:16], [0:512]} | slice | bytes 110592 | tf_op jit(solution)/shard_map/slice | solution.py:64
  90.7 1.5 %collective-permute-start.3 = (f32[3,3,3,3,1,512]{5,4,3,2,1,0:T(1,128)S(1)}, f32[3,3,3,3,1,512]{5,4,3,2,1,0:T(1,128)S(1)}, u32[]{:S(2)}, u32[]{:S(2)}) collective-permute-start(f32[3,3,3,3,1,512]{5,4,3,2,1,0:T(1,128)S(1)} %pad_maximum_fusion.5), channel_id=1, source_target_pairs={{0,1},{1,2},{2,3},{3,4},{4,5},{5,6},{6,7},{7,8},{8,9},{9,10},{10,1... | collective-permute-start | bytes 497672 | tf_op jit(solution)/shard_map/ppermute | solution.py:10
  92.2 1.1 %fusion.59 = f32[1,3,3,1,16,512]{5,4,2,1,3,0:T(8,128)S(1)} fusion(f32[3,3,3,1,16,512]{5,4,2,1,3,0:T(8,128)} %bitcast.31, f32[3,3,3,1,2,16,512]{6,5,2,1,4,3,0:T(8,128)S(1)} %maximum_select_fusion), kind=kLoop, calls=%fused_computation.119 | loop fusion | flops 368640 | bytes 1179648 | tf_op jit(solution)/shard_map/add | solution.py:57
  93.3 1.2 %fusion.50 = f32[1,3,3,1,16,512]{5,4,3,2,1,0:T(8,128)S(1)} fusion(f32[3,3,3,1,16,512]{5,4,3,2,1,0:T(8,128)} %collective-permute-done.2, f32[3,3,3,1,2,16,512]{6,5,2,1,4,3,0:T(8,128)S(1)} %maximum_select_fusion, f32[3,3,3,1,16,512]{5,4,2,1,3,0:T(8,128)} %bitcast.31), kind=kLoop, calls=%fused_computation.104 | loop fusion | flops 884736 | bytes 2359296 | tf_op jit(solution)/shard_map/add | solution.py:57
  94.5 0.3 stack.63
  95.9 1.0 slice_bitcast_fusion.4
  97.4 0.5 pad_maximum_fusion.3
  97.9 1.1 %fusion.67 = (f32[3,1,3,1,8,512]{5,3,4,2,1,0:T(1,128)S(1)}, f32[3,1,3,1,8,512]{5,3,4,2,1,0:T(1,128)S(1)}, f32[3,1,3,1,8,512]{5,3,4,2,1,0:T(1,128)S(1)}) fusion(f32[3,3,3,1,8,512]{5,3,4,2,1,0:T(1,128)S(1)} %pad_maximum_fusion.3, f32[3,3,3,1,8,512]{5,3,4,2,1,0:T(1,128)S(1)} %get-tuple-element.16, f32[3,3,3,1,8,512]{5,3,4,2,1,0:T(1,128)S(1)} %get-tuple-element.17), kind=kLoop, calls=%fused_computation.137 | loop fusion | flops 663552 | bytes 1769472 | tf_op jit(solution)/shard_map/add | solution.py:57
  99.1 0.8 and_select_fusion
  99.9 0.8 copy.60
  (52 shorter events, 3.6 us)
Async XLA Ops:
  11.3 4.4 %copy-start = (f32[3,3,3,4,32,512]{5,0,4,3,2,1:T(4,128)}, f32[3,3,3,4,32,512]{5,0,4,3,2,1:T(4,128)S(1)}, u32[]{:S(2)}) copy-start(f32[3,3,3,4,32,512]{5,0,4,3,2,1:T(4,128)S(1)} %copy_select_fusion) | copy-start | bytes 21233668
  13.5 36.8 %collective-permute-start = (f32[3,3,3,1,32,512]{5,0,4,3,2,1:T(4,128)}, f32[3,3,3,1,32,512]{5,0,4,3,2,1:T(4,128)}, u32[]{:S(2)}, u32[]{:S(2)}) collective-permute-start(f32[3,3,3,1,32,512]{5,0,4,3,2,1:T(4,128)} %slice.374), channel_id=1, source_target_pairs={{0,16},{16,32},{32,48},{48,64},{64,80},{80,96},{96,112},{112,128},... | collective-permute-start | bytes 5308424 | tf_op jit(solution)/shard_map/ppermute | solution.py:10
  19.6 49.4 %copy-start.3 = (pred[16]{0:T(512)(128)(4,1)}, pred[16]{0:T(512)(128)(4,1)S(1)}, u32[]{:S(2)}) copy-start(pred[16]{0:T(512)(128)(4,1)S(1)} %get-tuple-element.26) | copy-start | bytes 52
  19.6 49.4 %copy-start.4 = (pred[16]{0:T(512)(128)(4,1)}, pred[16]{0:T(512)(128)(4,1)S(1)}, u32[]{:S(2)}) copy-start(pred[16]{0:T(512)(128)(4,1)S(1)} %get-tuple-element.27) | copy-start | bytes 52
  51.3 15.9 %collective-permute-start.1 = (f32[3,3,3,5,1,512]{5,0,4,3,2,1:T(4,128)S(1)}, f32[3,3,3,5,1,512]{5,0,4,3,2,1:T(4,128)S(1)}, u32[]{:S(2)}, u32[]{:S(2)}) collective-permute-start(f32[3,3,3,5,1,512]{5,0,4,3,2,1:T(4,128)S(1)} %pad_maximum_fusion.4), channel_id=1, source_target_pairs={{0,1},{1,2},{2,3},{3,4},{4,5},{5,6},{6,7},{7,8},{8,9},{9,10},{10,1... | collective-permute-start | bytes 829448 | tf_op jit(solution)/shard_map/ppermute | solution.py:10
  69.5 5.4 %copy-start.1 = (f32[3,3,3,2,16,512]{5,4,3,2,1,0:T(8,128)}, f32[3,3,3,2,16,512]{5,4,3,2,1,0:T(8,128)S(1)}, u32[]{:S(2)}) copy-start(f32[3,3,3,2,16,512]{5,4,3,2,1,0:T(8,128)S(1)} %copy_select_fusion.1) | copy-start | bytes 5308420
  70.6 18.8 %collective-permute-start.2 = (f32[3,3,3,1,16,512]{5,4,3,2,1,0:T(8,128)}, f32[3,3,3,1,16,512]{5,4,3,2,1,0:T(8,128)}, u32[]{:S(2)}, u32[]{:S(2)}) collective-permute-start(f32[3,3,3,1,16,512]{5,4,3,2,1,0:T(8,128)} %slice.408), channel_id=1, source_target_pairs={{0,16},{16,32},{32,48},{48,64},{64,80},{80,96},{96,112},{112,128},... | collective-permute-start | bytes 2654216 | tf_op jit(solution)/shard_map/ppermute | solution.py:10
  76.1 14.5 %copy-start.2 = (f32[3,3,3,2,1,512]{5,4,3,2,1,0:T(1,128)S(1)}, f32[3,3,3,2,1,512]{5,4,3,2,1,0:T(1,128)}, u32[]{:S(2)}) copy-start(f32[3,3,3,2,1,512]{5,4,3,2,1,0:T(1,128)} %slice.410) | copy-start | bytes 331780
  90.7 6.6 %collective-permute-start.3 = (f32[3,3,3,3,1,512]{5,4,3,2,1,0:T(1,128)S(1)}, f32[3,3,3,3,1,512]{5,4,3,2,1,0:T(1,128)S(1)}, u32[]{:S(2)}, u32[]{:S(2)}) collective-permute-start(f32[3,3,3,3,1,512]{5,4,3,2,1,0:T(1,128)S(1)} %pad_maximum_fusion.5), channel_id=1, source_target_pairs={{0,1},{1,2},{2,3},{3,4},{4,5},{5,6},{6,7},{7,8},{8,9},{9,10},{10,1... | collective-permute-start | bytes 497672 | tf_op jit(solution)/shard_map/ppermute | solution.py:10
  97.0 2.1 %copy-start.5 = (s32[8]{0:T(128)S(1)}, s32[8]{0:T(128)}, u32[]{:S(2)}) copy-start(s32[8]{0:T(128)} %iota_add_fusion.3) | copy-start | bytes 100
  97.0 2.1 %copy-start.6 = (pred[8]{0:T(512)(128)(4,1)S(1)}, pred[8]{0:T(512)(128)(4,1)}, u32[]{:S(2)}) copy-start(pred[8]{0:T(512)(128)(4,1)} %compare_and_fusion) | copy-start | bytes 28
  97.0 2.1 %copy-start.7 = (pred[3]{0:T(512)(128)(4,1)S(1)}, pred[3]{0:T(512)(128)(4,1)}, u32[]{:S(2)}) copy-start(pred[3]{0:T(512)(128)(4,1)} %get-tuple-element.28) | copy-start | bytes 13
  97.0 2.1 %copy-start.8 = (pred[3]{0:T(512)(128)(4,1)S(1)}, pred[3]{0:T(512)(128)(4,1)}, u32[]{:S(2)}) copy-start(pred[3]{0:T(512)(128)(4,1)} %get-tuple-element.29) | copy-start | bytes 13
where the time goes:
time: 102 us; the launch traced here: 101 us
  other arithmetic  41 us (40%)
  waiting for transfers between devices  36.4 us (36%)
  local copies, waits for them, and re-layouts  15.5 us (15%)
  starting transfers between devices  6.61 us (6%)
  between operations  1.21 us (1%)
    ppermute x4, waiting for transfers between devices, from_behind(): lax.ppermute(value, axis, [(source, source + steps) for source in range(i...  36.4 us
    add x9, other arithmetic, coarsen_pairs(): total = term if total is None else total + term  25.4 us
    select_n x4, other arithmetic, boundary_mask(): return jnp.where(inside, coeffs, jnp.zeros_like(coeffs))  13.1 us
    ppermute x4, starting transfers between devices, from_behind(): lax.ppermute(value, axis, [(source, source + steps) for source in range(i...  6.61 us
    slice x6, local copies, waits for them, and re-layouts, last_rows(): return lax.slice_in_dim(values, length - width, length, 1, dim)  6.1 us
    squeeze x1, local copies, waits for them, and re-layouts, coarsen_pairs(): odd_rows = lax.index_in_dim(paired, 1, sdim + 1, keepdims=False)  3.16 us
  transfers between devices with their start and end apart: 4, of which 2 were waited for; matrix products, arithmetic and copies ran while one was open for 34% of the time, Pallas kernels for 0%

commit v1 on v0

v1 whole, which is shorter than its diff:
```python
import jax
import jax.numpy as jnp
from jax import lax
from jax.experimental import pallas as pl
from jax.experimental.pallas import tpu as pltpu
from jax.sharding import PartitionSpec as P

MESH = pl.DeviceIdType.MESH
F32 = jnp.float32
TOP = 8


def odd_parts(minus, centre, plus):
    half = 0.5 * centre
    return minus + half, half + plus


def even_parts(minus, centre, plus):
    return minus, minus + (centre + centre) + plus, plus


def transfer_kernel(
    n_x, n_y, z_run, stencil, level, second, fine, p_out, p_in, q_out, q_in, y_out, y_in, d_out, d_in,
    load_sem, p_send, p_recv, q_send, q_recv, edge_send, edge_recv, ready,
):
    gx, gy = lax.axis_index("gx"), lax.axis_index("gy")
    rows, nz = stencil.shape[4], stencil.shape[5]
    half, quarter = rows // 2, rows // 4
    chunks = nz // 128
    units = 3 * chunks
    fine_unit, level_unit = TOP + rows, TOP + half
    has_next_x, has_next_y = gx < n_x - 1, gy < n_y - 1
    has_prev_x, has_prev_y = gx > 0, gy > 0
    run_start, run_end = lax.rem(gy, z_run) == 0, lax.rem(gy, z_run) == z_run - 1

    def load(x, u):
        lanes = pl.ds(pl.multiple_of(u // 3 * 128, 128), 128)
        return pltpu.make_async_copy(
            stencil.at[:, :, lax.rem(u, 3), x, :, lanes],
            fine.at[x, :, :, pl.ds(pl.multiple_of(u * fine_unit + TOP, 8), rows), :],
            load_sem.at[x, u],
        )

    def over(count, body):
        def step(i, carry):
            body(i)
            return carry

        lax.fori_loop(0, count, step, 0)

    for x in (3, 1, 2, 0):
        over(units, lambda u: load(x, u).start())

    barrier = pltpu.get_barrier_semaphore()

    def tell(condition, x, y):
        @pl.when(condition)
        def _():
            pl.semaphore_signal(barrier, inc=1, device_id=(x, y), device_id_type=MESH)

    tell(has_prev_x, gx - 1, gy)
    tell(has_next_y & ~run_end, gx, gy + 1)
    tell(has_next_y & ~run_end & has_next_x, gx + 1, gy + 1)
    tell(has_prev_y & run_start, gx, gy - 1)
    tell(has_prev_y & run_start & has_prev_x, gx - 1, gy - 1)

    def p_part(u):
        return pl.ds(pl.multiple_of(u * half, 8), half)

    def s_part(u):
        return pl.ds(pl.multiple_of(u * quarter, 8), quarter)

    def inner(u):
        return pl.ds(pl.multiple_of(u * level_unit + TOP, 8), half)

    zero_row = jnp.zeros((1, 128), F32)

    def clear_fine(u, carry):
        for ox in range(3):
            for oy in range(3):
                for x in range(4):
                    fine[x, ox, oy, pl.ds(u * fine_unit + TOP - 1, 1), :] = zero_row
                for i_x in range(2):
                    level[i_x, ox, oy, pl.ds(u * level_unit + TOP - 1, 1), :] = zero_row
        return carry

    lax.fori_loop(0, units, clear_fine, 0)

    @pl.when(~has_prev_x)
    def _():
        def clear(u, carry):
            for ox in range(2):
                for oy in range(3):
                    p_in[ox, oy, p_part(u)] = jnp.zeros((half, 128), F32)
            q_in[u] = jnp.zeros(q_in.shape[1:], F32)
            return carry

        lax.fori_loop(0, units, clear, 0)

    @pl.when(~has_prev_y)
    def _():
        y_in[...] = jnp.zeros(y_in.shape, F32)

    @pl.when(~(has_prev_x & has_prev_y))
    def _():
        d_in[...] = jnp.zeros(d_in.shape, F32)

    row16 = lax.broadcasted_iota(jnp.int32, (half, 128), 0)
    row8 = lax.broadcasted_iota(jnp.int32, (quarter, 128), 0)
    keep_first = jnp.where((row16 == 0) & ~has_prev_y, 0.0, 1.0).astype(F32)
    keep_last = jnp.where((row16 == half - 1) & ~has_next_y, 0.0, 1.0).astype(F32)
    keep_last2 = jnp.where((row8 == quarter - 1) & ~has_next_y, 0.0, 1.0).astype(F32)
    keep_x0 = jnp.where(has_prev_x, 1.0, 0.0).astype(F32)
    keep_x1 = jnp.where(has_next_x, 1.0, 0.0).astype(F32)

    def outside_z(chunk, oz, lane):
        first = (oz == 0) & (chunk == 0) & (lane == 0)
        return first | ((oz == 2) & (chunk == chunks - 1) & (lane == 127))

    def quarter_z(u):
        lane = lax.broadcasted_iota(jnp.int32, (1, 128), 1)
        return jnp.where(outside_z(u // 3, lax.rem(u, 3), lane), 0.0, 0.25).astype(F32)

    def fold(read, keep_low, keep_high):
        before, behind = odd_parts(*(read(oy, TOP - 1) for oy in range(3)))
        ahead_0, ahead_1 = odd_parts(*(read(oy, TOP + 1) for oy in range(3)))
        own = [read(oy, TOP) for oy in range(3)]
        if keep_low is not None:
            own[0] = own[0] * keep_low
        e_minus, e_zero, e_plus = even_parts(*own)
        return before + e_minus, behind + e_zero + ahead_0, (e_plus + ahead_1) * keep_high

    def fold_fine(u, ox, x):
        def read(oy, first):
            return fine[x, ox, oy, pl.ds(u * fine_unit + first, half, stride=2), :]

        return fold(read, keep_first, keep_last)

    def fold_level(u, ox, i_x):
        def read(oy, first):
            return level[i_x, ox, oy, pl.ds(u * level_unit + first, quarter, stride=2), :]

        return fold(read, None, keep_last2)

    def send_p(c):
        part = pl.ds(pl.multiple_of(c * 3 * half, 8), 3 * half)
        return pltpu.make_async_remote_copy(
            p_out.at[:, :, part], p_in.at[:, :, part], p_send.at[c], p_recv.at[c], device_id=(gx + 1, gy), device_id_type=MESH
        )

    def p_unit(u):
        load(3, u).wait()
        scale = quarter_z(u)
        f = [fold_fine(u, ox, 3) for ox in range(3)]
        for oy in range(3):
            a, b = odd_parts(f[0][oy], f[1][oy], f[2][oy])
            p_out[0, oy, p_part(u)] = a * scale
            p_out[1, oy, p_part(u)] = b * scale

    def p_step(c):
        over(3, lambda oz: p_unit(c * 3 + oz))

        @pl.when(c == 0)
        def _():
            waits = (
                has_next_x.astype(jnp.int32)
                + (has_prev_y & ~run_start).astype(jnp.int32)
                + (has_prev_y & ~run_start & has_prev_x).astype(jnp.int32)
                + (has_next_y & run_end).astype(jnp.int32)
                + (has_next_y & run_end & has_next_x).astype(jnp.int32)
            )

            @pl.when(waits > 0)
            def _():
                pl.semaphore_wait(barrier, waits)

        @pl.when(has_next_x)
        def _():
            send_p(c).start()

    over(chunks, p_step)

    @pl.when(has_prev_y & ~run_start)
    def _():
        pl.semaphore_signal(ready.at[0], inc=1, device_id=(gx, gy - 1), device_id_type=MESH)

    @pl.when(has_prev_y & ~run_start & has_prev_x)
    def _():
        pl.semaphore_signal(ready.at[1], inc=1, device_id=(gx - 1, gy - 1), device_id_type=MESH)

    def second_row(u):
        load(1, u).wait()
        load(2, u).wait()
        scale = quarter_z(u)
        f1 = [fold_fine(u, ox, 1) for ox in range(3)]
        f2 = [fold_fine(u, ox, 2) for ox in range(3)]
        for oy in range(3):
            a, b = odd_parts(f1[0][oy], f1[1][oy], f1[2][oy])
            e = even_parts(f2[0][oy], f2[1][oy], f2[2][oy])
            level[0, 1, oy, inner(u), :] = a * scale
            level[0, 2, oy, inner(u), :] = b * scale
            level[1, 0, oy, inner(u), :] = (a + e[0]) * scale
            level[1, 1, oy, inner(u), :] = (b + e[1]) * scale + p_out[0, oy, p_part(u)]
            level[1, 2, oy, inner(u), :] = (e[2] * scale + p_out[1, oy, p_part(u)]) * keep_x1

    over(units, second_row)

    def first_row(u):
        load(0, u).wait()
        scale = quarter_z(u)
        f = [fold_fine(u, ox, 0) for ox in range(3)]
        for oy in range(3):
            e = even_parts(f[0][oy] * keep_x0, f[1][oy], f[2][oy])
            level[0, 0, oy, inner(u), :] = e[0] * scale
            level[0, 1, oy, inner(u), :] += e[1] * scale
            level[0, 2, oy, inner(u), :] += e[2] * scale

    over(units, first_row)

    def fine_edge(x, ox, oy):
        return fine[x, ox, oy, pl.ds(fine_unit - 1, units, stride=fine_unit), :]

    def level_at(row):
        return pl.ds(TOP + row, units, stride=level_unit)

    def p_edge(ox, oy):
        return p_out[ox, oy, pl.ds(half - 1, units, stride=half), :]

    def group(i):
        return pl.ds(i * units, units)

    unit = lax.broadcasted_iota(jnp.int32, (units, 128), 0)
    lane = lax.broadcasted_iota(jnp.int32, (units, 128), 1)
    scale = jnp.where(outside_z(unit // 3, lax.rem(unit, 3), lane), 0.0, 0.25).astype(F32)
    h = [[odd_parts(*(fine_edge(x, ox, oy) for oy in range(3))) for ox in range(3)] for x in range(4)]
    ahead = []
    for oy in range(2):
        a3, b3 = odd_parts(*(h[3][ox][oy] for ox in range(3)))
        a1, b1 = odd_parts(*(h[1][ox][oy] for ox in range(3)))
        e2 = even_parts(*(h[2][ox][oy] for ox in range(3)))
        e0 = even_parts(h[0][0][oy] * keep_x0, h[0][1][oy], h[0][2][oy])
        d_out[group(oy), :] = a3 * scale
        d_out[group(2 + oy), :] = b3 * scale
        y_out[group(oy), :] = e0[0] * scale
        y_out[group(2 + oy), :] = (e0[1] + a1) * scale
        y_out[group(4 + oy), :] = (e0[2] + b1) * scale
        ahead.append([(a1 + e2[0]) * scale, (b1 + e2[1] + a3) * scale, (e2[2] + b3) * scale * keep_x1])
        for ox in range(3):
            y_out[group(6 + ox * 2 + oy), :] = ahead[oy][ox]
    g = [
        [odd_parts(*(level[i_x, ox, oy, level_at(half - 1), :] for oy in range(3))) for ox in range(3)]
        for i_x in range(2)
    ]
    behind = [odd_parts(*(p_edge(ox, oy) for oy in range(3))) for ox in range(2)]
    onto = [odd_parts(*(ahead[oy][ox] for ox in range(3))) for oy in range(2)]
    for oy in range(2):
        a, b = odd_parts(*(g[1][ox][oy] for ox in range(3)))
        e = even_parts(*(g[0][ox][oy] for ox in range(3)))
        y_out[group(12 + oy), :] = e[0] * 0.25
        y_out[group(14 + oy), :] = (e[1] + a) * 0.25
        y_out[group(16 + oy), :] = (e[2] + b) * (0.25 * keep_x1)
        p_minus = behind[0][oy]
        p_zero = behind[0][oy] + (behind[1][oy] + behind[1][oy])
        onto_y = [onto[0][k] if oy == 0 else onto[0][k] + (onto[1][k] + onto[1][k]) for k in range(2)]
        d_out[group(4 + oy), :] = (a + p_minus + onto_y[0]) * 0.25
        d_out[group(6 + oy), :] = (b + p_zero + onto_y[1]) * 0.25

    send_y = pltpu.make_async_remote_copy(
        y_out, y_in, edge_send.at[0], edge_recv.at[0], device_id=(gx, gy + 1), device_id_type=MESH
    )
    send_d = pltpu.make_async_remote_copy(
        d_out, d_in, edge_send.at[1], edge_recv.at[1], device_id=(gx + 1, gy + 1), device_id_type=MESH
    )

    @pl.when(has_next_y)
    def _():
        @pl.when(~run_end)
        def _():
            pl.semaphore_wait(ready.at[0], 1)

        send_y.start()

    @pl.when(has_next_x & has_next_y)
    def _():
        @pl.when(~run_end)
        def _():
            pl.semaphore_wait(ready.at[1], 1)

        send_d.start()

    def send_q(c):
        part = pl.ds(c * 3, 3)
        return pltpu.make_async_remote_copy(
            q_out.at[part], q_in.at[part], q_send.at[c], q_recv.at[c], device_id=(gx + 1, gy), device_id_type=MESH
        )

    def q_unit(u):
        f = [fold_level(u, ox, 1) for ox in range(3)]
        for oy in range(3):
            a, b = odd_parts(f[0][oy], f[1][oy], f[2][oy])
            q_out[u, 0, oy] = a * 0.25
            q_out[u, 1, oy] = b * 0.25

    def q_step(c):
        over(3, lambda oz: q_unit(c * 3 + oz))

        @pl.when(has_next_x)
        def _():
            send_q(c).start()

    over(chunks, q_step)

    @pl.when(has_prev_y)
    def _():
        send_y.wait_recv()

    @pl.when(has_prev_x & has_prev_y)
    def _():
        send_d.wait_recv()

    for i_x in range(2):
        for ox in range(3):
            for oy in range(2):
                value = y_in[group(i_x * 6 + ox * 2 + oy), :]
                if i_x == 0 and ox < 2:
                    value = value + d_in[group(ox * 2 + oy), :]
                level[i_x, ox, oy, level_at(0), :] = level[i_x, ox, oy, level_at(0), :] + value

    def finish_one(u):
        for oy in range(3):
            for ox in range(2):
                level[0, ox, oy, inner(u), :] += p_in[ox, oy, p_part(u)]
        f0 = [fold_level(u, ox, 0) for ox in range(3)]
        f1 = [fold_level(u, ox, 1) for ox in range(3)]
        for oy in range(3):
            e = even_parts(f0[0][oy], f0[1][oy], f0[2][oy])
            a, b = odd_parts(f1[0][oy], f1[1][oy], f1[2][oy])
            second[0, oy, s_part(u)] = e[0] * 0.25
            second[1, oy, s_part(u)] = (e[1] + a) * 0.25
            second[2, oy, s_part(u)] = (e[2] + b) * (0.25 * keep_x1)

    def finish_one_step(c):
        @pl.when(has_prev_x)
        def _():
            send_p(c).wait_recv()

        over(3, lambda oz: finish_one(c * 3 + oz))

    over(chunks, finish_one_step)

    for ox in range(3):
        for oy in range(2):
            value = y_in[group(12 + ox * 2 + oy), :]
            if ox < 2:
                value = value + d_in[group(4 + ox * 2 + oy), :]
            at = pl.ds(0, units, stride=quarter)
            second[ox, oy, at, :] = second[ox, oy, at, :] + value

    def finish_two_step(c):
        @pl.when(has_prev_x)
        def _():
            send_q(c).wait_recv()

        for oz in range(3):
            for ox in range(2):
                for oy in range(3):
                    second[ox, oy, s_part(c * 3 + oz)] += q_in[c * 3 + oz, ox, oy]

    over(chunks, finish_two_step)

    @pl.when(has_next_x)
    def _():
        for c in range(chunks):
            send_p(c).wait_send()
            send_q(c).wait_send()

    @pl.when(has_next_y)
    def _():
        send_y.wait_send()

    @pl.when(has_next_x & has_next_y)
    def _():
        send_d.wait_send()


def write_kernel(level, second, one, two, sem):
    half, quarter, chunks = one.shape[4], two.shape[4], one.shape[5] // 128
    copies = []
    for u in range(3 * chunks):
        oz, lanes = u % 3, pl.ds(u // 3 * 128, 128)
        for i_x in range(2):
            source = level.at[i_x, :, :, pl.ds(u * (TOP + half) + TOP, half), :]
            copies.append(pltpu.make_async_copy(source, one.at[:, :, oz, i_x, :, lanes], sem.at[u, i_x]))
        source = second.at[:, :, pl.ds(u * quarter, quarter), :]
        copies.append(pltpu.make_async_copy(source, two.at[:, :, oz, 0, :, lanes], sem.at[u, 2]))
    for copy in copies:
        copy.start()
    for copy in copies:
        copy.wait()


def solution(mesh):
    n_x, n_y = mesh.shape["gx"], mesh.shape["gy"]
    z_run = n_y // 2

    def shard(stencil):
        _, _, _, cells_x, rows, nz = stencil.shape
        half, quarter, chunks = rows // 2, rows // 4, nz // 128
        units = 3 * chunks
        vmem, hbm = pl.BlockSpec(memory_space=pltpu.VMEM), pl.BlockSpec(memory_space=pl.ANY)

        def kernel(*refs):
            transfer_kernel(n_x, n_y, z_run, *refs)

        level, second = pl.pallas_call(
            kernel,
            out_shape=(
                pltpu.VMEM((2, 3, 3, units * (TOP + half), 128), F32),
                pltpu.VMEM((3, 3, units * quarter, 128), F32),
            ),
            in_specs=[hbm],
            out_specs=(vmem, vmem),
            scratch_shapes=[
                pltpu.VMEM((cells_x, 3, 3, units * (TOP + rows), 128), F32),
                pltpu.VMEM((2, 3, units * half, 128), F32),
                pltpu.VMEM((2, 3, units * half, 128), F32),
                pltpu.VMEM((units, 2, 3, quarter, 128), F32),
                pltpu.VMEM((units, 2, 3, quarter, 128), F32),
                pltpu.VMEM((18 * units, 128), F32),
                pltpu.VMEM((18 * units, 128), F32),
                pltpu.VMEM((8 * units, 128), F32),
                pltpu.VMEM((8 * units, 128), F32),
                pltpu.SemaphoreType.DMA((cells_x, units)),
                pltpu.SemaphoreType.DMA((chunks,)),
                pltpu.SemaphoreType.DMA((chunks,)),
                pltpu.SemaphoreType.DMA((chunks,)),
                pltpu.SemaphoreType.DMA((chunks,)),
                pltpu.SemaphoreType.DMA((2,)),
                pltpu.SemaphoreType.DMA((2,)),
                pltpu.SemaphoreType.REGULAR((2,)),
            ],
            compiler_params=pltpu.CompilerParams(
                collective_id=0, has_side_effects=True, vmem_limit_bytes=56 * 2**20
            ),
        )(stencil)
        return pl.pallas_call(
            write_kernel,
            out_shape=(
                jax.ShapeDtypeStruct((3, 3, 3, cells_x // 2, half, nz), F32),
                jax.ShapeDtypeStruct((3, 3, 3, cells_x // 4, quarter, nz), F32),
            ),
            in_specs=[vmem, vmem],
            out_specs=(hbm, hbm),
            scratch_shapes=[pltpu.SemaphoreType.DMA((units, 3))],
        )(level, second)

    spec = P(None, None, None, "gx", "gy", None)
    return jax.shard_map(shard, mesh=mesh, in_specs=(spec,), out_specs=(spec, spec), check_vma=False)
```

time: 102 us -> 25.9 us (0.25); the launches traced: 101 us -> 25.8 us
  other arithmetic: 41 us -> 0 us
  waiting for transfers between devices: 36.4 us -> 0 us
  Pallas kernels: 0 us -> 22.8 us
  local copies, waits for them, and re-layouts: 15.5 us -> 2.28 us
  starting transfers between devices: 6.61 us -> 0 us
    ppermute x4 -> x0, waiting for transfers between devices: 36.4 us -> none  [from_behind(): lax.ppermute(value, axis, [(source, source + steps) for source in range(i...]
    add x14 -> x0, other arithmetic: 26 us -> none  [the longest x9 25.4 us: coarsen_pairs(): total = term if total is None else total + term]
    pallas_call x0 -> x2, Pallas kernels: none -> 22.8 us  [the longest x1 19.4 us: shard(): pl.pallas_call(kernel, out_shape=(pltpu.VMEM((2, 3, 3, units * (TOP + hal...]
    select_n x4 -> x0, other arithmetic: 13.1 us -> none  [boundary_mask(): return jnp.where(inside, coeffs, jnp.zeros_like(coeffs))]
    slice x13 -> x0, local copies, waits for them, and re-layouts: 7.28 us -> none  [the longest x6 6.1 us: last_rows(): return lax.slice_in_dim(values, length - width, length, 1, dim)]
    ppermute x4 -> x0, starting transfers between devices: 6.61 us -> none  [from_behind(): lax.ppermute(value, axis, [(source, source + steps) for source in range(i...]
    squeeze x3 -> x0, local copies, waits for them, and re-layouts: 4.6 us -> none  [the longest x1 3.16 us: coarsen_pairs(): odd_rows = lax.index_in_dim(paired, 1, sdim + 1, keepdims=False)]
    another operation x5 -> x0, local copies, waits for them, and re-layouts: 1.24 us -> none  [coarsen_pairs(): return jnp.stack(results, axis=odim)]
  transfers between devices with their start and end apart: 4 -> 0, of which waited for: 2 -> 0; matrix products, arithmetic and copies ran while one was open for 34% -> 0% of each run, Pallas kernels for 0% -> 0%
where the time goes in v1:
time: 25.9 us; the launch traced here: 25.8 us
  Pallas kernels  22.8 us (88%)
  local copies, waits for them, and re-layouts  2.28 us (9%)
  between operations  0.65 us (3%)
    pallas_call x1, Pallas kernels, shard(): pl.pallas_call(kernel, out_shape=(pltpu.VMEM((2, 3, 3, units * (TOP + hal...  19.4 us
    pallas_call x1, Pallas kernels, shard(): pl.pallas_call(write_kernel, out_shape=(jax.ShapeDtypeStruct((3, 3, 3, ce...  3.46 us
    unnamed x4, local copies, waits for them, and re-layouts  2.28 us

profile of v1, /device:TPU:6, one launch (start us, length us, event | category | flops | bytes accessed | tf_op | source)
XLA Modules:
  0.0 25.8 jit_solution(5092560073823635121)
XLA Ops:
  0.6 19.4 %shard_map.30 = (f32[2,3,3,288,128]{4,3,2,1,0:T(8,128)S(1)}, f32[3,3,96,128]{3,2,1,0:T(8,128)S(1)}) custom-call(f32[3,3,3,4,32,512]{5,4,3,2,1,0:T(8,128)} %refs_0_.1), custom_call_target="tpu_custom_call" | custom-call | tf_op jit(solution)/shard_map/pallas_call | solution.py:415
  20.0 0.0 copy-start
  20.0 1.5 %copy-done = f32[2,3,3,288,128]{4,3,2,1,0:T(8,128)} copy-done((f32[2,3,3,288,128]{4,3,2,1,0:T(8,128)}, f32[2,3,3,288,128]{4,3,2,1,0:T(8,128)S(1)}, u32[]{:S(2)}) %copy-start) | copy-done | bytes 2654232
  21.5 0.0 copy-start.1
  21.5 0.8 %copy-done.1 = f32[3,3,96,128]{3,2,1,0:T(8,128)} copy-done((f32[3,3,96,128]{3,2,1,0:T(8,128)}, f32[3,3,96,128]{3,2,1,0:T(8,128)S(1)}, u32[]{:S(2)}) %copy-start.1) | copy-done | bytes 442392
  22.3 3.5 %shard_map.31 = (f32[3,3,3,2,16,512]{5,4,3,2,1,0:T(8,128)}, f32[3,3,3,1,8,512]{5,4,3,2,1,0:T(8,128)}) custom-call(f32[2,3,3,288,128]{4,3,2,1,0:T(8,128)} %copy-done, f32[3,3,96,128]{3,2,1,0:T(8,128)} %copy-done.1), custom_call_target="tpu_custom_call" | custom-call | tf_op jit(solution)/shard_map/pallas_call | solution.py:446
Async XLA Ops:
  20.0 1.5 %copy-start = (f32[2,3,3,288,128]{4,3,2,1,0:T(8,128)}, f32[2,3,3,288,128]{4,3,2,1,0:T(8,128)S(1)}, u32[]{:S(2)}) copy-start(f32[2,3,3,288,128]{4,3,2,1,0:T(8,128)S(1)} %get-tuple-element.4.level) | copy-start | bytes 7962628
  21.5 0.8 %copy-start.1 = (f32[3,3,96,128]{3,2,1,0:T(8,128)}, f32[3,3,96,128]{3,2,1,0:T(8,128)S(1)}, u32[]{:S(2)}) copy-start(f32[3,3,96,128]{3,2,1,0:T(8,128)S(1)} %get-tuple-element.5.second) | copy-start | bytes 1327108

commit v2 on v1

v2 whole, which is shorter than its diff:
```python
import jax
import jax.numpy as jnp
from jax import lax
from jax.experimental import pallas as pl
from jax.experimental.pallas import tpu as pltpu
from jax.sharding import PartitionSpec as P

MESH = pl.DeviceIdType.MESH
F32 = jnp.float32
TOP = 8


def odd_parts(minus, centre, plus):
    half = 0.5 * centre
    return minus + half, half + plus


def even_parts(minus, centre, plus):
    return minus, minus + (centre + centre) + plus, plus


def transfer_kernel(
    n_x, n_y, z_run, stencil, level, second, fine, p_out, p_in, q_out, q_in, y_out, y_in, d_out, d_in,
    load_sem, edge_sem, p_send, p_recv, q_send, q_recv, edge_send, edge_recv, ready,
):
    gx, gy = lax.axis_index("gx"), lax.axis_index("gy")
    rows, nz = stencil.shape[4], stencil.shape[5]
    half, quarter = rows // 2, rows // 4
    chunks = nz // 128
    fine_unit, level_unit = TOP + rows, TOP + half
    has_next_x, has_next_y = gx < n_x - 1, gy < n_y - 1
    has_prev_x, has_prev_y = gx > 0, gy > 0
    run_start, run_end = lax.rem(gy, z_run) == 0, lax.rem(gy, z_run) == z_run - 1

    def load(x, c, first, count, sem):
        lanes = pl.ds(pl.multiple_of(c * 128, 128), 128)
        return pltpu.make_async_copy(
            stencil.at[:, :, :, x, pl.ds(first, count), lanes],
            fine.at[x, :, :, :, pl.ds(pl.multiple_of(c * fine_unit + TOP + first, 8), count), :],
            sem,
        )

    def load_last_x(c):
        return load(3, c, 0, rows, load_sem.at[3, c])

    def load_body(x, c):
        return load(x, c, 0, rows - 8, load_sem.at[x, c])

    def load_edge(x, c):
        return load(x, c, rows - 8, 8, edge_sem.at[x, c])

    def over(count, body):
        def step(i, carry):
            body(i)
            return carry

        lax.fori_loop(0, count, step, 0)

    over(chunks, lambda c: load_last_x(c).start())

    barrier = pltpu.get_barrier_semaphore()

    def tell(condition, x, y):
        @pl.when(condition)
        def _():
            pl.semaphore_signal(barrier, inc=1, device_id=(x, y), device_id_type=MESH)

    tell(has_prev_x, gx - 1, gy)
    tell(has_next_y & ~run_end, gx, gy + 1)
    tell(has_next_y & ~run_end & has_next_x, gx + 1, gy + 1)
    tell(has_prev_y & run_start, gx, gy - 1)
    tell(has_prev_y & run_start & has_prev_x, gx - 1, gy - 1)

    def inner(c):
        return pl.ds(pl.multiple_of(c * level_unit + TOP, 8), half)

    def s_part(c):
        return pl.ds(pl.multiple_of(c * quarter, 8), quarter)

    zero_row = jnp.zeros((1, 128), F32)

    def clear_fine(x):
        def clear(c):
            for ox in range(3):
                for oy in range(3):
                    for oz in range(3):
                        fine[x, ox, oy, oz, pl.ds(c * fine_unit + TOP - 1, 1), :] = zero_row

        over(chunks, clear)

    def clear_level(c):
        for ox in range(3):
            for oy in range(3):
                for oz in range(3):
                    for i_x in range(2):
                        level[i_x, ox, oy, oz, pl.ds(c * level_unit + TOP - 1, 1), :] = zero_row

    clear_fine(3)

    @pl.when(~has_prev_x)
    def _():
        def clear(c):
            p_in[c] = jnp.zeros(p_in.shape[1:], F32)
            q_in[c] = jnp.zeros(q_in.shape[1:], F32)

        over(chunks, clear)

    @pl.when(~has_prev_y)
    def _():
        y_in[...] = jnp.zeros(y_in.shape, F32)

    @pl.when(~(has_prev_x & has_prev_y))
    def _():
        d_in[...] = jnp.zeros(d_in.shape, F32)

    row16 = lax.broadcasted_iota(jnp.int32, (half, 128), 0)
    row8 = lax.broadcasted_iota(jnp.int32, (quarter, 128), 0)
    keep_first = jnp.where((row16 == 0) & ~has_prev_y, 0.0, 1.0).astype(F32)
    keep_last = jnp.where((row16 == half - 1) & ~has_next_y, 0.0, 1.0).astype(F32)
    keep_last2 = jnp.where((row8 == quarter - 1) & ~has_next_y, 0.0, 1.0).astype(F32)
    keep_x0 = jnp.where(has_prev_x, 1.0, 0.0).astype(F32)
    keep_x1 = jnp.where(has_next_x, 1.0, 0.0).astype(F32)

    def quarter_z(c, oz, row_is_chunk=False):
        lane = lax.broadcasted_iota(jnp.int32, (chunks if row_is_chunk else 1, 128), 1)
        if row_is_chunk:
            c = lax.broadcasted_iota(jnp.int32, (chunks, 128), 0)
        outside = ((oz == 0) & (c == 0) & (lane == 0)) | ((oz == 2) & (c == chunks - 1) & (lane == 127))
        return jnp.where(outside, 0.0, 0.25).astype(F32)

    def fold(read, keep_low, keep_high):
        before, behind = odd_parts(*(read(oy, TOP - 1) for oy in range(3)))
        ahead_0, ahead_1 = odd_parts(*(read(oy, TOP + 1) for oy in range(3)))
        own = [read(oy, TOP) for oy in range(3)]
        if keep_low is not None:
            own[0] = own[0] * keep_low
        e_minus, e_zero, e_plus = even_parts(*own)
        return before + e_minus, behind + e_zero + ahead_0, (e_plus + ahead_1) * keep_high

    def fold_fine(c, oz, ox, x):
        def read(oy, first):
            return fine[x, ox, oy, oz, pl.ds(c * fine_unit + first, half, stride=2), :]

        return fold(read, keep_first, keep_last)

    def fold_level(c, oz, ox, i_x):
        def read(oy, first):
            return level[i_x, ox, oy, oz, pl.ds(c * level_unit + first, quarter, stride=2), :]

        return fold(read, None, keep_last2)

    def over_z(body):
        def step(oz, carry):
            body(oz)
            return carry

        lax.fori_loop(0, 3, step, 0)

    def send_p(c):
        return pltpu.make_async_remote_copy(
            p_out.at[c], p_in.at[c], p_send.at[c], p_recv.at[c], device_id=(gx + 1, gy), device_id_type=MESH
        )

    def p_step(c):
        load_last_x(c).wait()

        def unit(oz):
            scale = quarter_z(c, oz)
            f = [fold_fine(c, oz, ox, 3) for ox in range(3)]
            for oy in range(3):
                a, b = odd_parts(f[0][oy], f[1][oy], f[2][oy])
                p_out[c, 0, oy, oz] = a * scale
                p_out[c, 1, oy, oz] = b * scale

        over_z(unit)

        @pl.when(c == 0)
        def _():
            waits = (
                has_next_x.astype(jnp.int32)
                + (has_prev_y & ~run_start).astype(jnp.int32)
                + (has_prev_y & ~run_start & has_prev_x).astype(jnp.int32)
                + (has_next_y & run_end).astype(jnp.int32)
                + (has_next_y & run_end & has_next_x).astype(jnp.int32)
            )

            @pl.when(waits > 0)
            def _():
                pl.semaphore_wait(barrier, waits)

        @pl.when(has_next_x)
        def _():
            send_p(c).start()

        @pl.when(c == 0)
        def _():
            for x in range(3):
                over(chunks, lambda c: load_edge(x, c).start())

    over(chunks, p_step)

    for x in (1, 2, 0):
        over(chunks, lambda c: load_body(x, c).start())

    @pl.when(has_prev_y & ~run_start)
    def _():
        pl.semaphore_signal(ready.at[0], inc=1, device_id=(gx, gy - 1), device_id_type=MESH)

    @pl.when(has_prev_y & ~run_start & has_prev_x)
    def _():
        pl.semaphore_signal(ready.at[1], inc=1, device_id=(gx - 1, gy - 1), device_id_type=MESH)

    for x in range(3):
        clear_fine(x)
    over(chunks, clear_level)

    def group(i, oz):
        return pl.ds((i * 3 + oz) * chunks, chunks)

    def fold_last(oz, ox, x):
        def read(oy, back):
            return fine[x, ox, oy, oz, pl.ds(fine_unit - back, chunks, stride=fine_unit), :]

        before, behind = odd_parts(*(read(oy, 3) for oy in range(3)))
        ahead = odd_parts(*(read(oy, 1) for oy in range(3)))
        e = even_parts(*(read(oy, 2) for oy in range(3)))
        return (before + e[0], behind + e[1] + ahead[0], e[2] + ahead[1]), ahead

    def edges(oz):
        scale = quarter_z(None, oz, True)
        f = [[fold_last(oz, ox, x) for ox in range(3)] for x in range(4)]

        def across(parts):
            a3, b3 = odd_parts(*parts[3])
            a1, b1 = odd_parts(*parts[1])
            e2 = even_parts(*parts[2])
            e0 = even_parts(parts[0][0] * keep_x0, parts[0][1], parts[0][2])
            first = [e0[0] * scale, (e0[1] + a1) * scale, (e0[2] + b1) * scale]
            second_x = [(a1 + e2[0]) * scale, (b1 + e2[1] + a3) * scale, (e2[2] + b3) * scale * keep_x1]
            return first, second_x, [a3 * scale, b3 * scale]

        onto = []
        for oy in range(2):
            first, second_x, beyond = across([[f[x][ox][1][oy] for ox in range(3)] for x in range(4)])
            onto.append(odd_parts(*second_x))
            for ox in range(3):
                y_out[group(ox * 2 + oy, oz), :] = first[ox]
                y_out[group(6 + ox * 2 + oy, oz), :] = second_x[ox]
            for ox in range(2):
                d_out[group(ox * 2 + oy, oz), :] = beyond[ox]
        own = [across([[f[x][ox][0][oy] for ox in range(3)] for x in range(4)]) for oy in range(3)]
        g = [[odd_parts(*(own[oy][i][ox] for oy in range(3))) for ox in range(3 if i < 2 else 2)] for i in range(3)]
        for oy in range(2):
            a, b = odd_parts(*(g[1][ox][oy] for ox in range(3)))
            e = even_parts(*(g[0][ox][oy] for ox in range(3)))
            y_out[group(12 + oy, oz), :] = e[0] * 0.25
            y_out[group(14 + oy, oz), :] = (e[1] + a) * 0.25
            y_out[group(16 + oy, oz), :] = (e[2] + b) * (0.25 * keep_x1)
            p_minus = g[2][0][oy]
            p_zero = g[2][0][oy] + (g[2][1][oy] + g[2][1][oy])
            onto_y = [onto[0][k] if oy == 0 else onto[0][k] + (onto[1][k] + onto[1][k]) for k in range(2)]
            d_out[group(4 + oy, oz), :] = (a + p_minus + onto_y[0]) * 0.25
            d_out[group(6 + oy, oz), :] = (b + p_zero + onto_y[1]) * 0.25

    for x in range(3):
        over(chunks, lambda c: load_edge(x, c).wait())
    over_z(edges)

    send_y = pltpu.make_async_remote_copy(
        y_out, y_in, edge_send.at[0], edge_recv.at[0], device_id=(gx, gy + 1), device_id_type=MESH
    )
    send_d = pltpu.make_async_remote_copy(
        d_out, d_in, edge_send.at[1], edge_recv.at[1], device_id=(gx + 1, gy + 1), device_id_type=MESH
    )

    def send_edges(condition):
        @pl.when(condition & has_next_y)
        def _():
            @pl.when(~run_end)
            def _():
                pl.semaphore_wait(ready.at[0], 1)

            send_y.start()

        @pl.when(condition & has_next_x & has_next_y)
        def _():
            @pl.when(~run_end)
            def _():
                pl.semaphore_wait(ready.at[1], 1)

            send_d.start()

    send_edges(~run_start)

    def second_row(c):
        load_body(1, c).wait()
        load_body(2, c).wait()

        def unit(oz):
            scale = quarter_z(c, oz)
            f1 = [fold_fine(c, oz, ox, 1) for ox in range(3)]
            f2 = [fold_fine(c, oz, ox, 2) for ox in range(3)]
            for oy in range(3):
                a, b = odd_parts(f1[0][oy], f1[1][oy], f1[2][oy])
                e = even_parts(f2[0][oy], f2[1][oy], f2[2][oy])
                level[0, 1, oy, oz, inner(c), :] = a * scale
                level[0, 2, oy, oz, inner(c), :] = b * scale
                level[1, 0, oy, oz, inner(c), :] = (a + e[0]) * scale
                level[1, 1, oy, oz, inner(c), :] = (b + e[1]) * scale + p_out[c, 0, oy, oz]
                level[1, 2, oy, oz, inner(c), :] = (e[2] * scale + p_out[c, 1, oy, oz]) * keep_x1

        over_z(unit)

    over(chunks, second_row)

    def send_q(c):
        return pltpu.make_async_remote_copy(
            q_out.at[c], q_in.at[c], q_send.at[c], q_recv.at[c], device_id=(gx + 1, gy), device_id_type=MESH
        )

    def q_step(c):
        def unit(oz):
            f = [fold_level(c, oz, ox, 1) for ox in range(3)]
            for oy in range(3):
                a, b = odd_parts(f[0][oy], f[1][oy], f[2][oy])
                q_out[c, 0, oy, oz] = a * 0.25
                q_out[c, 1, oy, oz] = b * 0.25

        over_z(unit)

        @pl.when(has_next_x)
        def _():
            send_q(c).start()

    over(chunks, q_step)

    def first_row(c):
        load_body(0, c).wait()

        def unit(oz):
            scale = quarter_z(c, oz)
            f = [fold_fine(c, oz, ox, 0) for ox in range(3)]
            for oy in range(3):
                e = even_parts(f[0][oy] * keep_x0, f[1][oy], f[2][oy])
                level[0, 0, oy, oz, inner(c), :] = e[0] * scale
                level[0, 1, oy, oz, inner(c), :] += e[1] * scale
                level[0, 2, oy, oz, inner(c), :] += e[2] * scale

        over_z(unit)

    over(chunks, first_row)

    send_edges(run_start)

    @pl.when(has_prev_y)
    def _():
        send_y.wait_recv()

    @pl.when(has_prev_x & has_prev_y)
    def _():
        send_d.wait_recv()

    def add_edges(oz):
        at = pl.ds(TOP, chunks, stride=level_unit)
        for i_x in range(2):
            for ox in range(3):
                for oy in range(2):
                    value = y_in[group(i_x * 6 + ox * 2 + oy, oz), :]
                    if i_x == 0 and ox < 2:
                        value = value + d_in[group(ox * 2 + oy, oz), :]
                    level[i_x, ox, oy, oz, at, :] = level[i_x, ox, oy, oz, at, :] + value

    over_z(add_edges)

    def finish_one(c):
        @pl.when(has_prev_x)
        def _():
            send_p(c).wait_recv()

        def unit(oz):
            for oy in range(3):
                for ox in range(2):
                    level[0, ox, oy, oz, inner(c), :] += p_in[c, ox, oy, oz]
            f0 = [fold_level(c, oz, ox, 0) for ox in range(3)]
            f1 = [fold_level(c, oz, ox, 1) for ox in range(3)]
            for oy in range(3):
                e = even_parts(f0[0][oy], f0[1][oy], f0[2][oy])
                a, b = odd_parts(f1[0][oy], f1[1][oy], f1[2][oy])
                second[0, oy, oz, s_part(c), :] = e[0] * 0.25
                second[1, oy, oz, s_part(c), :] = (e[1] + a) * 0.25
                second[2, oy, oz, s_part(c), :] = (e[2] + b) * (0.25 * keep_x1)

        over_z(unit)

    over(chunks, finish_one)

    def add_edges_two(oz):
        at = pl.ds(0, chunks, stride=quarter)
        for ox in range(3):
            for oy in range(2):
                value = y_in[group(12 + ox * 2 + oy, oz), :]
                if ox < 2:
                    value = value + d_in[group(4 + ox * 2 + oy, oz), :]
                second[ox, oy, oz, at, :] = second[ox, oy, oz, at, :] + value

    over_z(add_edges_two)

    def finish_two(c):
        @pl.when(has_prev_x)
        def _():
            send_q(c).wait_recv()

        for oz in range(3):
            for ox in range(2):
                for oy in range(3):
                    second[ox, oy, oz, s_part(c), :] += q_in[c, ox, oy, oz]

    over(chunks, finish_two)

    @pl.when(has_next_x)
    def _():
        for c in range(chunks):
            send_p(c).wait_send()
            send_q(c).wait_send()

    @pl.when(has_next_y)
    def _():
        send_y.wait_send()

    @pl.when(has_next_x & has_next_y)
    def _():
        send_d.wait_send()


def write_kernel(level, second, one, two, sem):
    half, quarter, chunks = one.shape[4], two.shape[4], one.shape[5] // 128
    copies = []
    for c in range(chunks):
        lanes = pl.ds(c * 128, 128)
        for i_x in range(2):
            source = level.at[i_x, :, :, :, pl.ds(c * (TOP + half) + TOP, half), :]
            copies.append(pltpu.make_async_copy(source, one.at[:, :, :, i_x, :, lanes], sem.at[c, i_x]))
        source = second.at[:, :, :, pl.ds(c * quarter, quarter), :]
        copies.append(pltpu.make_async_copy(source, two.at[:, :, :, 0, :, lanes], sem.at[c, 2]))
    for copy in copies:
        copy.start()
    for copy in copies:
        copy.wait()


def solution(mesh):
    n_x, n_y = mesh.shape["gx"], mesh.shape["gy"]
    z_run = n_y // 2

    def shard(stencil):
        _, _, _, cells_x, rows, nz = stencil.shape
        half, quarter, chunks = rows // 2, rows // 4, nz // 128
        vmem, hbm = pl.BlockSpec(memory_space=pltpu.VMEM), pl.BlockSpec(memory_space=pl.ANY)

        def kernel(*refs):
            transfer_kernel(n_x, n_y, z_run, *refs)

        level, second = pl.pallas_call(
            kernel,
            out_shape=(
                pltpu.VMEM((2, 3, 3, 3, chunks * (TOP + half), 128), F32),
                pltpu.VMEM((3, 3, 3, chunks * quarter, 128), F32),
            ),
            in_specs=[hbm],
            out_specs=(vmem, vmem),
            scratch_shapes=[
                pltpu.VMEM((cells_x, 3, 3, 3, chunks * (TOP + rows), 128), F32),
                pltpu.VMEM((chunks, 2, 3, 3, half, 128), F32),
                pltpu.VMEM((chunks, 2, 3, 3, half, 128), F32),
                pltpu.VMEM((chunks, 2, 3, 3, quarter, 128), F32),
                pltpu.VMEM((chunks, 2, 3, 3, quarter, 128), F32),
                pltpu.VMEM((54 * chunks, 128), F32),
                pltpu.VMEM((54 * chunks, 128), F32),
                pltpu.VMEM((24 * chunks, 128), F32),
                pltpu.VMEM((24 * chunks, 128), F32),
                pltpu.SemaphoreType.DMA((cells_x, chunks)),
                pltpu.SemaphoreType.DMA((cells_x - 1, chunks)),
                pltpu.SemaphoreType.DMA((chunks,)),
                pltpu.SemaphoreType.DMA((chunks,)),
                pltpu.SemaphoreType.DMA((chunks,)),
                pltpu.SemaphoreType.DMA((chunks,)),
                pltpu.SemaphoreType.DMA((2,)),
                pltpu.SemaphoreType.DMA((2,)),
                pltpu.SemaphoreType.REGULAR((2,)),
            ],
            compiler_params=pltpu.CompilerParams(
                collective_id=0, has_side_effects=True, vmem_limit_bytes=56 * 2**20
            ),
        )(stencil)
        level, second = (pltpu.with_memory_space_constraint(v, pltpu.VMEM) for v in (level, second))
        return pl.pallas_call(
            write_kernel,
            out_shape=(
                jax.ShapeDtypeStruct((3, 3, 3, cells_x // 2, half, nz), F32),
                jax.ShapeDtypeStruct((3, 3, 3, cells_x // 4, quarter, nz), F32),
            ),
            in_specs=[vmem, vmem],
            out_specs=(hbm, hbm),
            scratch_shapes=[pltpu.SemaphoreType.DMA((chunks, 3))],
            compiler_params=pltpu.CompilerParams(vmem_limit_bytes=2**20),
        )(level, second)

    spec = P(None, None, None, "gx", "gy", None)
    return jax.shard_map(shard, mesh=mesh, in_specs=(spec,), out_specs=(spec, spec), check_vma=False)
```

time: 25.9 us -> 20.7 us (0.80)
  Pallas kernels: 22.8 us -> 19.9 us
  local copies, waits for them, and re-layouts: 2.28 us -> 0 us
    unnamed x4 -> x0, local copies, waits for them, and re-layouts: 2.28 us -> none
    pallas_call x1, Pallas kernels: 3.46 us -> 1.45 us  [shard(): pl.pallas_call(write_kernel, out_shape=(jax.ShapeDtypeStruct((3, 3, 3, ce...]
    pallas_call x1, Pallas kernels: 19.4 us -> 18.4 us  [shard(): pl.pallas_call(kernel, out_shape=(pltpu.VMEM((2, 3, 3, 3, chunks * (TOP +...]
where the time goes in v2:
time: 20.7 us; the launch traced here: 20.5 us
  Pallas kernels  19.9 us (96%)
  between operations  0.64 us (3%)
    pallas_call x1, Pallas kernels, shard(): pl.pallas_call(kernel, out_shape=(pltpu.VMEM((2, 3, 3, 3, chunks * (TOP +...  18.4 us
    pallas_call x1, Pallas kernels, shard(): pl.pallas_call(write_kernel, out_shape=(jax.ShapeDtypeStruct((3, 3, 3, ce...  1.45 us

profile of v2, /device:TPU:6, one launch (start us, length us, event | category | flops | bytes accessed | tf_op | source)
XLA Modules:
  0.0 20.5 jit_solution(13064643666657675549)
XLA Ops:
  0.6 18.4 %shard_map.30 = (f32[2,3,3,3,96,128]{5,4,3,2,1,0:T(8,128)S(1)}, f32[3,3,3,32,128]{4,3,2,1,0:T(8,128)S(1)}) custom-call(f32[3,3,3,4,32,512]{5,4,3,2,1,0:T(8,128)} %refs_0_.1), custom_call_target="tpu_custom_call" | custom-call | tf_op jit(solution)/shard_map/pallas_call | solution.py:463
  19.1 1.4 %shard_map.31 = (f32[3,3,3,2,16,512]{5,4,3,2,1,0:T(8,128)}, f32[3,3,3,1,8,512]{5,4,3,2,1,0:T(8,128)}) custom-call(f32[2,3,3,3,96,128]{5,4,3,2,1,0:T(8,128)S(1)} %get-tuple-element.4.level, f32[3,3,3,32,128]{4,3,2,1,0:T(8,128)S(1)} %get-tuple-element.5.second), custom_call_target="tpu_custom_call" | custom-call | tf_op jit(solution)/shard_map/pallas_call | solution.py:496

commit v3 on v2

--- a/solution.py
+++ b/solution.py
@@ -20,8 +20,8 @@
 
 
 def transfer_kernel(
-    n_x, n_y, z_run, stencil, level, second, fine, p_out, p_in, q_out, q_in, y_out, y_in, d_out, d_in,
-    load_sem, edge_sem, p_send, p_recv, q_send, q_recv, edge_send, edge_recv, ready,
+    n_x, n_y, z_run, stencil, level, second, fine, p_out, p_in, q_out, q_in, y_out, y_in, d_out, d_in, q_relay,
+    load_sem, edge_sem, p_send, p_recv, q_send, q_recv, edge_send, edge_recv, relay_sem, ready,
 ):
     gx, gy = lax.axis_index("gx"), lax.axis_index("gy")
     rows, nz = stencil.shape[4], stencil.shape[5]
@@ -31,6 +31,16 @@
     has_next_x, has_next_y = gx < n_x - 1, gy < n_y - 1
     has_prev_x, has_prev_y = gx > 0, gy > 0
     run_start, run_end = lax.rem(gy, z_run) == 0, lax.rem(gy, z_run) == z_run - 1
+    first_core = lax.rem(gx, 2) == 0
+    second_core = ~first_core
+    giver = run_end & has_next_y
+    paced = giver & second_core & has_next_x
+    hand_late = giver & (gx == n_x - 2)
+    low_y = lax.rem(gx, 4) < 2
+    arrived_first = jnp.where(low_y, 1, 1)
+    sent_first = jnp.where(low_y, 1, 3)
+    detour = second_core & (gy == 0) & (lax.rem(gx, 4) == 1) & has_next_x
+    relay = first_core & (gy == 1) & (lax.rem(gx, 4) == 2) & has_prev_x
 
     def load(x, c, first, count, sem):
         lanes = pl.ds(pl.multiple_of(c * 128, 128), 128)
@@ -67,9 +77,9 @@
 
     tell(has_prev_x, gx - 1, gy)
     tell(has_next_y & ~run_end, gx, gy + 1)
-    tell(has_next_y & ~run_end & has_next_x, gx + 1, gy + 1)
+    tell(has_next_y & ~run_end & has_next_x & second_core, gx + 1, gy + 1)
     tell(has_prev_y & run_start, gx, gy - 1)
-    tell(has_prev_y & run_start & has_prev_x, gx - 1, gy - 1)
+    tell(has_prev_y & run_start & has_prev_x & first_core, gx - 1, gy - 1)
 
     def inner(c):
         return pl.ds(pl.multiple_of(c * level_unit + TOP, 8), half)
@@ -108,10 +118,6 @@
     @pl.when(~has_prev_y)
     def _():
         y_in[...] = jnp.zeros(y_in.shape, F32)
-
-    @pl.when(~(has_prev_x & has_prev_y))
-    def _():
-        d_in[...] = jnp.zeros(d_in.shape, F32)
 
     row16 = lax.broadcasted_iota(jnp.int32, (half, 128), 0)
     row8 = lax.broadcasted_iota(jnp.int32, (quarter, 128), 0)
@@ -179,15 +185,23 @@
             waits = (
                 has_next_x.astype(jnp.int32)
                 + (has_prev_y & ~run_start).astype(jnp.int32)
-                + (has_prev_y & ~run_start & has_prev_x).astype(jnp.int32)
+                + (has_prev_y & ~run_start & has_prev_x & first_core).astype(jnp.int32)
                 + (has_next_y & run_end).astype(jnp.int32)
-                + (has_next_y & run_end & has_next_x).astype(jnp.int32)
+                + (has_next_y & run_end & has_next_x & second_core).astype(jnp.int32)
             )
 
             @pl.when(waits > 0)
             def _():
                 pl.semaphore_wait(barrier, waits)
 
+                @pl.when(has_prev_y & ~run_start)
+                def _():
+                    pl.semaphore_signal(ready.at[0], inc=1, device_id=(gx, gy - 1), device_id_type=MESH)
+
+                @pl.when(has_prev_y & ~run_start & has_prev_x & first_core)
+                def _():
+                    pl.semaphore_signal(ready.at[1], inc=1, device_id=(gx - 1, gy - 1), device_id_type=MESH)
+
         @pl.when(has_next_x)
         def _():
             send_p(c).start()
@@ -201,14 +215,6 @@
 
     for x in (1, 2, 0):
         over(chunks, lambda c: load_body(x, c).start())
-
-    @pl.when(has_prev_y & ~run_start)
-    def _():
-        pl.semaphore_signal(ready.at[0], inc=1, device_id=(gx, gy - 1), device_id_type=MESH)
-
-    @pl.when(has_prev_y & ~run_start & has_prev_x)
-    def _():
-        pl.semaphore_signal(ready.at[1], inc=1, device_id=(gx - 1, gy - 1), device_id_type=MESH)
 
     for x in range(3):
         clear_fine(x)
@@ -269,28 +275,26 @@
     send_y = pltpu.make_async_remote_copy(
         y_out, y_in, edge_send.at[0], edge_recv.at[0], device_id=(gx, gy + 1), device_id_type=MESH
     )
-    send_d = pltpu.make_async_remote_copy(
-        d_out, d_in, edge_send.at[1], edge_recv.at[1], device_id=(gx + 1, gy + 1), device_id_type=MESH
-    )
-
-    def send_edges(condition):
-        @pl.when(condition & has_next_y)
-        def _():
-            @pl.when(~run_end)
-            def _():
-                pl.semaphore_wait(ready.at[0], 1)
-
-            send_y.start()
-
-        @pl.when(condition & has_next_x & has_next_y)
-        def _():
-            @pl.when(~run_end)
-            def _():
-                pl.semaphore_wait(ready.at[1], 1)
-
-            send_d.start()
-
-    send_edges(~run_start)
+    def copy_d(x, y, k):
+        return pltpu.make_async_remote_copy(
+            d_out, d_in, edge_send.at[k], edge_recv.at[k], device_id=(x, y), device_id_type=MESH
+        )
+
+    hand_d, send_d = copy_d(gx + 1, gy, 2), copy_d(gx + 1, gy + 1, 1)
+
+    @pl.when(first_core & has_next_y & ~hand_late)
+    def _():
+        hand_d.start()
+
+    @pl.when(second_core & run_end & has_next_x & has_next_y)
+    def _():
+        send_d.start()
+
+    def add_corner(ref):
+        for i in range(4):
+            for k in (0, 1):
+                to, at = pl.ds((i + 12 * k) * 3 * chunks, 3 * chunks), pl.ds((i + 4 * k) * 3 * chunks, 3 * chunks)
+                ref[to, :] = ref[to, :] + d_in[at, :]
 
     def second_row(c):
         load_body(1, c).wait()
@@ -318,6 +322,13 @@
             q_out.at[c], q_in.at[c], q_send.at[c], q_recv.at[c], device_id=(gx + 1, gy), device_id_type=MESH
         )
 
+    detour_q = pltpu.make_async_remote_copy(
+        q_out.at[0], q_relay, q_send.at[0], relay_sem.at[0], device_id=(gx + 1, gy + 1), device_id_type=MESH
+    )
+    relay_q = pltpu.make_async_remote_copy(
+        q_relay, q_in.at[0], relay_sem.at[1], q_recv.at[0], device_id=(gx, gy - 1), device_id_type=MESH
+    )
+
     def q_step(c):
         def unit(oz):
             f = [fold_level(c, oz, ox, 1) for ox in range(3)]
@@ -328,9 +339,14 @@
 
         over_z(unit)
 
-        @pl.when(has_next_x)
+        @pl.when(has_next_x & ~(detour & (c == 0)))
         def _():
             send_q(c).start()
+
+        @pl.when(detour & (c == 0))
+        def _():
+            pl.semaphore_wait(ready.at[1], 1)
+            detour_q.start()
 
     over(chunks, q_step)
 
@@ -350,27 +366,38 @@
 
     over(chunks, first_row)
 
-    send_edges(run_start)
-
-    @pl.when(has_prev_y)
-    def _():
-        send_y.wait_recv()
-
-    @pl.when(has_prev_x & has_prev_y)
-    def _():
-        send_d.wait_recv()
-
-    def add_edges(oz):
-        at = pl.ds(TOP, chunks, stride=level_unit)
-        for i_x in range(2):
-            for ox in range(3):
-                for oy in range(2):
-                    value = y_in[group(i_x * 6 + ox * 2 + oy, oz), :]
-                    if i_x == 0 and ox < 2:
-                        value = value + d_in[group(ox * 2 + oy, oz), :]
-                    level[i_x, ox, oy, oz, at, :] = level[i_x, ox, oy, oz, at, :] + value
-
-    over_z(add_edges)
+    for c in range(3):
+
+        @pl.when(paced & (c < sent_first))
+        def _():
+            send_p(c).wait_send()
+
+    @pl.when(second_core & has_next_y)
+    def _():
+        hand_d.wait_recv()
+        add_corner(y_out)
+
+    @pl.when(has_next_y & ~(giver & first_core & ~low_y))
+    def _():
+        @pl.when(~run_end)
+        def _():
+            pl.semaphore_wait(ready.at[0], 1)
+
+        send_y.start()
+
+
+    @pl.when(second_core & has_next_x & has_next_y & ~run_end)
+    def _():
+        @pl.when(~detour)
+        def _():
+            pl.semaphore_wait(ready.at[1], 1)
+
+        send_d.start()
+
+    @pl.when(relay)
+    def _():
+        detour_q.wait_recv()
+        relay_q.start()
 
     def finish_one(c):
         @pl.when(has_prev_x)
@@ -392,18 +419,48 @@
 
         over_z(unit)
 
+        @pl.when(giver & first_core & ~low_y & (c == arrived_first - 1))
+        def _():
+            send_y.start()
+
+        @pl.when(hand_late & (c == arrived_first - 1))
+        def _():
+            hand_d.start()
+
     over(chunks, finish_one)
 
-    def add_edges_two(oz):
-        at = pl.ds(0, chunks, stride=quarter)
+    def add_edges(oz):
+        one_at, two_at = pl.ds(TOP, chunks, stride=level_unit), pl.ds(0, chunks, stride=quarter)
+        e, o = [], []
+        for oy in range(2):
+            h = [[y_in[group(i_x * 6 + ox * 2 + oy, oz), :] for ox in range(3)] for i_x in range(2)]
+            for i_x in range(2):
+                for ox in range(3):
+                    level[i_x, ox, oy, oz, one_at, :] = level[i_x, ox, oy, oz, one_at, :] + h[i_x][ox]
+            e.append(even_parts(*h[0]))
+            o.append(odd_parts(*h[1]))
+        onto = [[e[oy][0], e[oy][1] + o[oy][0], (e[oy][2] + o[oy][1]) * keep_x1] for oy in range(2)]
         for ox in range(3):
-            for oy in range(2):
-                value = y_in[group(12 + ox * 2 + oy, oz), :]
-                if ox < 2:
-                    value = value + d_in[group(4 + ox * 2 + oy, oz), :]
-                second[ox, oy, oz, at, :] = second[ox, oy, oz, at, :] + value
-
-    over_z(add_edges_two)
+            minus, centre = onto[0][ox], onto[0][ox] + (onto[1][ox] + onto[1][ox])
+            for oy, value in ((0, minus), (1, centre)):
+                value = value * 0.25 + y_in[group(12 + ox * 2 + oy, oz), :]
+                second[ox, oy, oz, two_at, :] = second[ox, oy, oz, two_at, :] + value
+
+    def finish_edges():
+        send_y.wait_recv()
+
+        @pl.when(first_core & has_prev_x)
+        def _():
+            send_d.wait_recv()
+            add_corner(y_in)
+
+        over_z(add_edges)
+
+    taker = run_start & has_prev_y
+
+    @pl.when(has_prev_y & ~run_start)
+    def _():
+        finish_edges()
 
     def finish_two(c):
         @pl.when(has_prev_x)
@@ -417,19 +474,36 @@
 
     over(chunks, finish_two)
 
+    @pl.when(taker)
+    def _():
+        finish_edges()
+
     @pl.when(has_next_x)
     def _():
         for c in range(chunks):
+            send_q(c).wait_send()
+
+    @pl.when(relay)
+    def _():
+        relay_q.wait_send()
+
+    for c in range(chunks):
+
+        @pl.when(has_next_x & ~(paced & (c < sent_first)))
+        def _():
             send_p(c).wait_send()
-            send_q(c).wait_send()
 
     @pl.when(has_next_y)
     def _():
         send_y.wait_send()
 
-    @pl.when(has_next_x & has_next_y)
+    @pl.when(second_core & has_next_x & has_next_y)
     def _():
         send_d.wait_send()
+
+    @pl.when(first_core & has_next_y)
+    def _():
+        hand_d.wait_send()
 
 
 def write_kernel(level, second, one, two, sem):
@@ -478,13 +552,15 @@
                 pltpu.VMEM((54 * chunks, 128), F32),
                 pltpu.VMEM((24 * chunks, 128), F32),
                 pltpu.VMEM((24 * chunks, 128), F32),
+                pltpu.VMEM((2, 3, 3, quarter, 128), F32),
                 pltpu.SemaphoreType.DMA((cells_x, chunks)),
                 pltpu.SemaphoreType.DMA((cells_x - 1, chunks)),
                 pltpu.SemaphoreType.DMA((chunks,)),
                 pltpu.SemaphoreType.DMA((chunks,)),
                 pltpu.SemaphoreType.DMA((chunks,)),
                 pltpu.SemaphoreType.DMA((chunks,)),
-                pltpu.SemaphoreType.DMA((2,)),
+                pltpu.SemaphoreType.DMA((3,)),
+                pltpu.SemaphoreType.DMA((3,)),
                 pltpu.SemaphoreType.DMA((2,)),
                 pltpu.SemaphoreType.REGULAR((2,)),
             ],

time: 20.7 us -> 19.1 us (0.923)
  the two profiles are of different devices: /device:TPU:6 before, /device:TPU:31 now
where the time goes in v3:
time: 19.1 us; the launch traced here: 19 us
  Pallas kernels  18.3 us (96%)
  between operations  0.64 us (3%)
    pallas_call x1, Pallas kernels, shard(): pl.pallas_call(kernel, out_shape=(pltpu.VMEM((2, 3, 3, 3, chunks * (TOP +...  16.9 us
    pallas_call x1, Pallas kernels, shard(): pl.pallas_call(write_kernel, out_shape=(jax.ShapeDtypeStruct((3, 3, 3, ce...  1.45 us

profile of v3, /device:TPU:31, one launch (start us, length us, event | category | flops | bytes accessed | tf_op | source)
XLA Modules:
  0.0 19.0 jit_solution(13864963181200793564)
XLA Ops:
  0.6 16.9 %shard_map.30 = (f32[2,3,3,3,96,128]{5,4,3,2,1,0:T(8,128)S(1)}, f32[3,3,3,32,128]{4,3,2,1,0:T(8,128)S(1)}) custom-call(f32[3,3,3,4,32,512]{5,4,3,2,1,0:T(8,128)} %refs_0_.1), custom_call_target="tpu_custom_call" | custom-call | tf_op jit(solution)/shard_map/pallas_call | solution.py:537
  17.5 1.4 %shard_map.31 = (f32[3,3,3,2,16,512]{5,4,3,2,1,0:T(8,128)}, f32[3,3,3,1,8,512]{5,4,3,2,1,0:T(8,128)}) custom-call(f32[2,3,3,3,96,128]{5,4,3,2,1,0:T(8,128)S(1)} %get-tuple-element.4.level, f32[3,3,3,32,128]{4,3,2,1,0:T(8,128)S(1)} %get-tuple-element.5.second), custom_call_target="tpu_custom_call" | custom-call | tf_op jit(solution)/shard_map/pallas_call | solution.py:572

commit v4 on v3

--- a/solution.py
+++ b/solution.py
@@ -34,13 +34,15 @@
     first_core = lax.rem(gx, 2) == 0
     second_core = ~first_core
     giver = run_end & has_next_y
-    paced = giver & second_core & has_next_x
-    hand_late = giver & (gx == n_x - 2)
-    low_y = lax.rem(gx, 4) < 2
+    paced = giver & second_core & has_next_x & (gx != 3)
+    last = giver & (gx == n_x - 1)
+    low_y = (lax.rem(gx, 4) < 2) | (gx < 4)
     arrived_first = jnp.where(low_y, 1, 1)
-    sent_first = jnp.where(low_y, 1, 3)
+    sent_first = jnp.where((gx == 1) | ~low_y, 2, 1)
     detour = second_core & (gy == 0) & (lax.rem(gx, 4) == 1) & has_next_x
     relay = first_core & (gy == 1) & (lax.rem(gx, 4) == 2) & has_prev_x
+    half_detour = second_core & (gy == 0) & (lax.rem(gx, 4) == 3) & has_next_x
+    half_relay = first_core & (gy == 1) & (lax.rem(gx, 4) == 0) & has_prev_x
 
     def load(x, c, first, count, sem):
         lanes = pl.ds(pl.multiple_of(c * 128, 128), 128)
@@ -282,7 +284,7 @@
 
     hand_d, send_d = copy_d(gx + 1, gy, 2), copy_d(gx + 1, gy + 1, 1)
 
-    @pl.when(first_core & has_next_y & ~hand_late)
+    @pl.when(first_core & has_next_y)
     def _():
         hand_d.start()
 
@@ -329,6 +331,16 @@
         q_relay, q_in.at[0], relay_sem.at[1], q_recv.at[0], device_id=(gx, gy - 1), device_id_type=MESH
     )
 
+    half_detour_q = pltpu.make_async_remote_copy(
+        q_out.at[0, 0], q_relay.at[0], q_send.at[0], relay_sem.at[0], device_id=(gx + 1, gy + 1), device_id_type=MESH
+    )
+    half_relay_q = pltpu.make_async_remote_copy(
+        q_relay.at[0], q_in.at[0, 0], relay_sem.at[1], q_recv.at[0], device_id=(gx, gy - 1), device_id_type=MESH
+    )
+    half_direct_q = pltpu.make_async_remote_copy(
+        q_out.at[0, 1], q_in.at[0, 1], q_send.at[0], q_recv.at[0], device_id=(gx + 1, gy), device_id_type=MESH
+    )
+
     def q_step(c):
         def unit(oz):
             f = [fold_level(c, oz, ox, 1) for ox in range(3)]
@@ -339,7 +351,7 @@
 
         over_z(unit)
 
-        @pl.when(has_next_x & ~(detour & (c == 0)))
+        @pl.when(has_next_x & ~((detour | half_detour) & (c == 0)))
         def _():
             send_q(c).start()
 
@@ -347,6 +359,12 @@
         def _():
             pl.semaphore_wait(ready.at[1], 1)
             detour_q.start()
+
+        @pl.when(half_detour & (c == 0))
+        def _():
+            pl.semaphore_wait(ready.at[1], 1)
+            half_detour_q.start()
+            half_direct_q.start()
 
     over(chunks, q_step)
 
@@ -366,7 +384,7 @@
 
     over(chunks, first_row)
 
-    for c in range(3):
+    for c in range(2):
 
         @pl.when(paced & (c < sent_first))
         def _():
@@ -377,7 +395,7 @@
         hand_d.wait_recv()
         add_corner(y_out)
 
-    @pl.when(has_next_y & ~(giver & first_core & ~low_y))
+    @pl.when(has_next_y & ~(giver & first_core & ~low_y) & ~last & ~(giver & (gx == 0)))
     def _():
         @pl.when(~run_end)
         def _():
@@ -388,7 +406,7 @@
 
     @pl.when(second_core & has_next_x & has_next_y & ~run_end)
     def _():
-        @pl.when(~detour)
+        @pl.when(~(detour | half_detour))
         def _():
             pl.semaphore_wait(ready.at[1], 1)
 
@@ -398,6 +416,11 @@
     def _():
         detour_q.wait_recv()
         relay_q.start()
+
+    @pl.when(half_relay)
+    def _():
+        half_detour_q.wait_recv()
+        half_relay_q.start()
 
     def finish_one(c):
         @pl.when(has_prev_x)
@@ -423,11 +446,11 @@
         def _():
             send_y.start()
 
-        @pl.when(hand_late & (c == arrived_first - 1))
-        def _():
-            hand_d.start()
-
     over(chunks, finish_one)
+
+    @pl.when(last | (giver & (gx == 0)))
+    def _():
+        send_y.start()
 
     def add_edges(oz):
         one_at, two_at = pl.ds(TOP, chunks, stride=level_unit), pl.ds(0, chunks, stride=quarter)
@@ -486,6 +509,10 @@
     @pl.when(relay)
     def _():
         relay_q.wait_send()
+
+    @pl.when(half_relay)
+    def _():
+        half_relay_q.wait_send()
 
     for c in range(chunks):
 

time: 19.1 us -> 19 us (level)
  the two profiles are of different devices: /device:TPU:31 before, /device:TPU:6 now
where the time goes in v4:
time: 19 us; the launch traced here: 18.8 us
  Pallas kernels  18.2 us (96%)
  between operations  0.64 us (3%)
    pallas_call x1, Pallas kernels, shard(): pl.pallas_call(kernel, out_shape=(pltpu.VMEM((2, 3, 3, 3, chunks * (TOP +...  16.7 us
    pallas_call x1, Pallas kernels, shard(): pl.pallas_call(write_kernel, out_shape=(jax.ShapeDtypeStruct((3, 3, 3, ce...  1.45 us

profile of v4, /device:TPU:6, one launch (start us, length us, event | category | flops | bytes accessed | tf_op | source)
XLA Modules:
  0.0 18.8 jit_solution(10852085414145164984)
XLA Ops:
  0.6 16.7 %shard_map.30 = (f32[2,3,3,3,96,128]{5,4,3,2,1,0:T(8,128)S(1)}, f32[3,3,3,32,128]{4,3,2,1,0:T(8,128)S(1)}) custom-call(f32[3,3,3,4,32,512]{5,4,3,2,1,0:T(8,128)} %refs_0_.1), custom_call_target="tpu_custom_call" | custom-call | tf_op jit(solution)/shard_map/pallas_call | solution.py:564
  17.4 1.4 %shard_map.31 = (f32[3,3,3,2,16,512]{5,4,3,2,1,0:T(8,128)}, f32[3,3,3,1,8,512]{5,4,3,2,1,0:T(8,128)}) custom-call(f32[2,3,3,3,96,128]{5,4,3,2,1,0:T(8,128)S(1)} %get-tuple-element.4.level, f32[3,3,3,32,128]{4,3,2,1,0:T(8,128)S(1)} %get-tuple-element.5.second), custom_call_target="tpu_custom_call" | custom-call | tf_op jit(solution)/shard_map/pallas_call | solution.py:599

commit v5 on v4

--- a/solution.py
+++ b/solution.py
@@ -39,10 +39,10 @@
     low_y = (lax.rem(gx, 4) < 2) | (gx < 4)
     arrived_first = jnp.where(low_y, 1, 1)
     sent_first = jnp.where((gx == 1) | ~low_y, 2, 1)
-    detour = second_core & (gy == 0) & (lax.rem(gx, 4) == 1) & has_next_x
-    relay = first_core & (gy == 1) & (lax.rem(gx, 4) == 2) & has_prev_x
-    half_detour = second_core & (gy == 0) & (lax.rem(gx, 4) == 3) & has_next_x
-    half_relay = first_core & (gy == 1) & (lax.rem(gx, 4) == 0) & has_prev_x
+    detour = second_core & run_start & (lax.rem(gx, 4) == 1) & has_next_x
+    relay = first_core & (lax.rem(gy, z_run) == 1) & (lax.rem(gx, 4) == 2) & has_prev_x
+    half_detour = second_core & run_start & (lax.rem(gx, 4) == 3) & has_next_x
+    half_relay = first_core & (lax.rem(gy, z_run) == 1) & (lax.rem(gx, 4) == 0) & has_prev_x
 
     def load(x, c, first, count, sem):
         lanes = pl.ds(pl.multiple_of(c * 128, 128), 128)

time: 19 us -> 19 us (level)
  no operation moved by 1% of the time
where the time goes in v5:
time: 19 us; the launch traced here: 18.8 us
  Pallas kernels  18.2 us (96%)
  between operations  0.64 us (3%)
    pallas_call x1, Pallas kernels, shard(): pl.pallas_call(kernel, out_shape=(pltpu.VMEM((2, 3, 3, 3, chunks * (TOP +...  16.7 us
    pallas_call x1, Pallas kernels, shard(): pl.pallas_call(write_kernel, out_shape=(jax.ShapeDtypeStruct((3, 3, 3, ce...  1.45 us

profile of v5, /device:TPU:6, one launch (start us, length us, event | category | flops | bytes accessed | tf_op | source)
XLA Modules:
  0.0 18.8 jit_solution(6243301251530885666)
XLA Ops:
  0.6 16.7 %shard_map.30 = (f32[2,3,3,3,96,128]{5,4,3,2,1,0:T(8,128)S(1)}, f32[3,3,3,32,128]{4,3,2,1,0:T(8,128)S(1)}) custom-call(f32[3,3,3,4,32,512]{5,4,3,2,1,0:T(8,128)} %refs_0_.1), custom_call_target="tpu_custom_call" | custom-call | tf_op jit(solution)/shard_map/pallas_call | solution.py:564
  17.4 1.4 %shard_map.31 = (f32[3,3,3,2,16,512]{5,4,3,2,1,0:T(8,128)}, f32[3,3,3,1,8,512]{5,4,3,2,1,0:T(8,128)}) custom-call(f32[2,3,3,3,96,128]{5,4,3,2,1,0:T(8,128)S(1)} %get-tuple-element.4.level, f32[3,3,3,32,128]{4,3,2,1,0:T(8,128)S(1)} %get-tuple-element.5.second), custom_call_target="tpu_custom_call" | custom-call | tf_op jit(solution)/shard_map/pallas_call | solution.py:599

commit v6 on v3

--- a/solution.py
+++ b/solution.py
@@ -516,8 +516,8 @@
             copies.append(pltpu.make_async_copy(source, one.at[:, :, :, i_x, :, lanes], sem.at[c, i_x]))
         source = second.at[:, :, :, pl.ds(c * quarter, quarter), :]
         copies.append(pltpu.make_async_copy(source, two.at[:, :, :, 0, :, lanes], sem.at[c, 2]))
-    for copy in copies:
-        copy.start()
+    for i, copy in enumerate(copies):
+        copy.start(priority=i % 2)
     for copy in copies:
         copy.wait()
 

time: 19.1 us -> 19.1 us (level)
  no operation moved by 1% of the time
where the time goes in v6:
time: 19.1 us; the launch traced here: 19 us
  Pallas kernels  18.4 us (96%)
  between operations  0.64 us (3%)
    pallas_call x1, Pallas kernels, shard(): pl.pallas_call(kernel, out_shape=(pltpu.VMEM((2, 3, 3, 3, chunks * (TOP +...  16.9 us
    pallas_call x1, Pallas kernels, shard(): pl.pallas_call(write_kernel, out_shape=(jax.ShapeDtypeStruct((3, 3, 3, ce...  1.47 us

profile of v6, /device:TPU:31, one launch (start us, length us, event | category | flops | bytes accessed | tf_op | source)
XLA Modules:
  0.0 19.0 jit_solution(14654650217489639683)
XLA Ops:
  0.6 16.9 %shard_map.30 = (f32[2,3,3,3,96,128]{5,4,3,2,1,0:T(8,128)S(1)}, f32[3,3,3,32,128]{4,3,2,1,0:T(8,128)S(1)}) custom-call(f32[3,3,3,4,32,512]{5,4,3,2,1,0:T(8,128)} %refs_0_.1), custom_call_target="tpu_custom_call" | custom-call | tf_op jit(solution)/shard_map/pallas_call | solution.py:537
  17.5 1.5 %shard_map.31 = (f32[3,3,3,2,16,512]{5,4,3,2,1,0:T(8,128)}, f32[3,3,3,1,8,512]{5,4,3,2,1,0:T(8,128)}) custom-call(f32[2,3,3,3,96,128]{5,4,3,2,1,0:T(8,128)S(1)} %get-tuple-element.4.level, f32[3,3,3,32,128]{4,3,2,1,0:T(8,128)S(1)} %get-tuple-element.5.second), custom_call_target="tpu_custom_call" | custom-call | tf_op jit(solution)/shard_map/pallas_call | solution.py:572
